TPU v7x, 1024 devices: a whole 4x8x16 slice. The times are simulated.
1024 devices in a mesh: dp: 32 (over z, core), owner: 32 (over x, y).
Axes of the slice: x: 4, y: 8, z: 16, core: 2. Of those that a mesh axis runs over, the one named last changes fastest.
Arguments:
- grad_rows: bfloat16 [262144, 1024], P(('dp', 'owner')), may hold values from -6 to 6
- token_owner: int32 [262144], P(('dp', 'owner')), may hold values from 0 to 31, as said below
- token_slot: int32 [262144], P(('dp', 'owner')), may hold values from 0 to 39
- ngram_input: bfloat16 [40960, 1024], P(('dp', 'owner')), may hold values from -6 to 6
- up_weight: bfloat16 [1024, 4096], P(None, 'dp'), may hold values from -0.1875 to 0.1875
- down_weight: bfloat16 [4096, 1024], P('dp'), may hold values from -0.09375 to 0.09375
Outputs:
- grad_up: float32 [1024, 4096], P('owner', 'dp')
- grad_down: float32 [4096, 1024], P('dp', 'owner')
Inputs may be any that keep to these rules, and one draw needn't show every extreme that they name: `token_owner`: from the positions of one device at most 16 go to any one owner; in every data group one owner receives exactly 16 from every device of the group.
All inputs are finite; a program needn't handle non-finite values.
Results may differ from a plain program's by a relative error of at most 0.0041.
Values may be sent and summed in bfloat16 or wider, within the bound.
A program may use at most 32 MiB of HBM per device.

v0:
```python
import jax
import jax.numpy as jnp
from jax import lax
from jax.sharding import PartitionSpec as P


def block_terms(inputs, grads, up_weight, down_weight):
    pre = jnp.dot(inputs, up_weight, preferred_element_type=jnp.float32)
    act = jax.nn.gelu(pre).astype(jnp.bfloat16)
    d_act = lax.dot_general(
        grads, down_weight, (((1,), (1,)), ((), ())), preferred_element_type=jnp.float32
    )
    d_pre = jax.vjp(jax.nn.gelu, pre)[1](d_act)[0].astype(jnp.bfloat16)
    upper = lax.dot_general(
        inputs, d_pre, (((0,), (0,)), ((), ())), preferred_element_type=jnp.float32
    )
    lower = lax.dot_general(
        act, grads, (((0,), (0,)), ((), ())), preferred_element_type=jnp.float32
    )
    return (upper, lower)


def on_device(grad_rows, token_owner, token_slot, ngram_input, up_weight, down_weight):
    owners = lax.axis_size("owner")
    tok_count = grad_rows.shape[0]
    width = grad_rows.shape[1]
    capacity = 2 * tok_count // owners
    ngram_count = ngram_input.shape[0]
    hits = (token_owner[:, None] == jnp.arange(owners, dtype=jnp.int32)[None, :]).astype(jnp.int32)
    ranking = jnp.sum(jnp.cumsum(hits, axis=0) * hits, axis=1) - 1
    placing = token_owner * capacity + ranking
    send_rows = jnp.zeros((owners * capacity, width), jnp.bfloat16).at[placing].set(grad_rows)
    send_slots = jnp.zeros((owners * capacity,), jnp.int32).at[placing].set(token_slot + 1)
    got_rows, got_slots = (
        lax.all_to_all(
            send_rows.reshape(owners, capacity, width),
            "owner",
            split_axis=0,
            concat_axis=0,
            tiled=True,
        ),
        lax.all_to_all(
            send_slots.reshape(owners, capacity), "owner", split_axis=0, concat_axis=0, tiled=True
        ),
    )
    matching = (
        got_slots.reshape(-1)[None, :] == jnp.arange(1, ngram_count + 1, dtype=jnp.int32)[:, None]
    ).astype(jnp.bfloat16)
    ngram_grad = jnp.dot(
        matching, got_rows.reshape(-1, width), preferred_element_type=jnp.float32
    ).astype(jnp.bfloat16)
    partial_up, partial_down = block_terms(
        lax.all_gather(ngram_input, "dp", axis=0, tiled=True),
        lax.all_gather(ngram_grad, "dp", axis=0, tiled=True),
        up_weight,
        down_weight,
    )
    total_up, total_down = lax.psum((partial_up, partial_down), "owner")
    where = lax.axis_index("owner")
    share = width // owners
    grad_up = lax.dynamic_slice_in_dim(total_up, where * share, share, 0)
    grad_down = lax.dynamic_slice_in_dim(total_down, where * share, share, 1)
    return (grad_up, grad_down)


def solution(mesh):
    in_specs = (
        P(("dp", "owner"), None),
        P(("dp", "owner")),
        P(("dp", "owner")),
        P(("dp", "owner"), None),
        P(None, "dp"),
        P("dp", None),
    )
    out_specs = (P("owner", "dp"), P("dp", "owner"))
    return jax.shard_map(
        on_device, mesh=mesh, in_specs=in_specs, out_specs=out_specs, check_vma=False
    )
```

profile of v0, /device:TPU:1, one launch (start us, length us, event | category | flops | bytes accessed | tf_op | source)
XLA Modules:
  0.0 362.7 jit_solution(14751314792650611037)
XLA Ops:
  7.2 0.0 copy-start
  7.2 0.0 all-gather.5.cloned.1.call-start
  7.2 0.7 all-gather.5.cloned.1.call-update
  7.9 0.7 fusion.26
  8.6 0.6 reduce-window.6
  9.2 0.2 slice_reduce_fusion
  9.4 0.8 fusion.25
  10.2 0.7 compare_select_fusion
  10.9 1.4 scatter_custom_fusion
  12.3 0.7 all_to_all.9
  13.0 10.5 %all-to-all-start = ((s32[32,1,16]{2,1,0:T(1,128)}), s32[32,1,16]{2,1,0:T(1,128)S(1)}, u32[]{:S(2)}, u32[]{:S(2)}) async-start(s32[32,1,16]{2,1,0:T(1,128)} %bitcast.2), calls=%async_computation | async-start | bytes 32768 | tf_op jit(solution)/shard_map/all_to_all | solution.py:42
  23.5 3.2 scatter_custom_fusion.1
  26.7 5.4 %all-to-all-done = s32[32,1,16]{2,1,0:T(1,128)S(1)} async-done(((s32[32,1,16]{2,1,0:T(1,128)}), s32[32,1,16]{2,1,0:T(1,128)S(1)}, u32[]{:S(2)}, u32[]{:S(2)}) %all-to-all-start) | async-done | bytes 2080 | tf_op jit(solution)/shard_map/all_to_all | solution.py:42
  32.0 3.9 %all-to-all-start.1 = ((bf16[32,16,1024]{2,1,0:T(8,128)(2,1)}), bf16[32,16,1024]{2,1,0:T(8,128)(2,1)S(1)}, u32[]{:S(2)}, u32[]{:S(2)}) async-start(bf16[32,16,1024]{2,1,0:T(8,128)(2,1)} %bitcast.3), calls=%async_computation.1 | async-start | bytes 2097152 | tf_op jit(solution)/shard_map/all_to_all | solution.py:35
  36.0 0.0 all-gather.3.cloned.1.call-start
  36.0 0.5 broadcast.96
  36.6 0.7 reduce.5
  37.2 0.1 eq.45
  37.3 16.0 %all-to-all-done.1 = bf16[32,16,1024]{2,1,0:T(8,128)(2,1)S(1)} async-done(((bf16[32,16,1024]{2,1,0:T(8,128)(2,1)}), bf16[32,16,1024]{2,1,0:T(8,128)(2,1)S(1)}, u32[]{:S(2)}, u32[]{:S(2)}) %all-to-all-start.1) | async-done | bytes 1048608 | tf_op jit(solution)/shard_map/all_to_all | solution.py:35
  53.3 1.0 convolution_convert_fusion
  54.3 0.0 all-gather.3.cloned.1.call-update
  54.3 0.0 all-reduce.3.cloned.1.call-start
  54.4 41.8 %all-gather.5.cloned.1.call-done = bf16[1280,1024]{1,0:T(8,128)(2,1)} async-done(((bf16[40,1024]{1,0:T(8,128)(2,1)}), bf16[1280,1024]{1,0:T(8,128)(2,1)}) %all-gather.5.cloned.1.call-update) | async-done | bytes 2621456 | tf_op jit(solution)/shard_map/all_gather | solution.py:53
  96.2 0.0 copy-done
  96.2 2.6 fusion.41
  98.8 0.0 copy-start.1
  98.8 72.5 %all-gather.3.cloned.1.call-done = bf16[1280,1024]{1,0:T(8,128)(2,1)} async-done(((bf16[40,1024]{1,0:T(8,128)(2,1)}), bf16[1280,1024]{1,0:T(8,128)(2,1)}) %all-gather.3.cloned.1.call-update) | async-done | bytes 2621456 | tf_op jit(solution)/shard_map/all_gather | solution.py:54
  171.2 3.7 %fusion.9 = f32[128,1024]{0,1:T(8,128)} fusion(bf16[1280,1024]{1,0:T(8,128)(2,1)} %all-gather.3.cloned.1.call-done, f32[1280,128]{1,0:T(8,128)S(1)} %fusion.41), kind=kOutput, calls=%fused_computation.16 | convolution fusion | flops 337018880 | bytes 3801088 | tf_op jit(solution)/shard_map/dot_general | solution.py:17
  174.9 0.0 copy-done.1
  174.9 4.4 %convolution_bitcast_fusion = f32[1024,128]{0,1:T(8,128)} fusion(bf16[1280,1024]{1,0:T(8,128)(2,1)S(1)} %copy-done.1, f32[1280,128]{1,0:T(8,128)S(1)} %fusion.41, bf16[1280,1024]{1,0:T(8,128)(2,1)} %all-gather.3.cloned.1.call-done, bf16[128,1024]{1,0:T(8,128)(2,1)} %param.11), kind=kOutput, calls=%fused_computation.2 | convolution fusion | flops 674365440 | bytes 6684672 | tf_op jit(solution)/shard_map/dot_general | solution.py:14
  179.4 0.0 all-reduce.3.cloned.1.call-update
  179.4 173.9 %all-reduce.3.cloned.1.call-done = (f32[1024,128]{0,1:T(8,128)}, f32[128,1024]{0,1:T(8,128)}) async-done(((f32[1024,128]{0,1:T(8,128)}, f32[128,1024]{0,1:T(8,128)}), (f32[1024,128]{0,1:T(8,128)}, f32[128,1024]{0,1:T(8,128)})) %all-reduce.3.cloned.1.call-update) | async-done | bytes 1048592 | tf_op jit(solution)/shard_map/psum | solution.py:58
  353.2 0.9 constant_dynamic-slice_fusion.1
  354.2 0.7 copy.13
  354.8 1.3 constant_dynamic-slice_fusion
  (3 shorter events, 0.0 us)
Async XLA Ops:
  7.2 89.0 %copy-start = (bf16[1024,128]{1,0:T(8,128)(2,1)S(1)}, bf16[1024,128]{1,0:T(8,128)(2,1)}, u32[]{:S(2)}) copy-start(bf16[1024,128]{1,0:T(8,128)(2,1)} %param.10) | copy-start | bytes 786436
  7.2 89.0 %all-gather.5.cloned.1.call-start = ((), (), s32[]{:S(2)}) async-start(), calls=%async_computation.3 | async-start | bytes 2703360 | tf_op jit(solution)/shard_map/all_gather | solution.py:53
  13.0 19.1 %all-to-all-start = ((s32[32,1,16]{2,1,0:T(1,128)}), s32[32,1,16]{2,1,0:T(1,128)S(1)}, u32[]{:S(2)}, u32[]{:S(2)}) async-start(s32[32,1,16]{2,1,0:T(1,128)} %bitcast.2), calls=%async_computation | async-start | bytes 32768 | tf_op jit(solution)/shard_map/all_to_all | solution.py:42
  32.0 21.3 %all-to-all-start.1 = ((bf16[32,16,1024]{2,1,0:T(8,128)(2,1)}), bf16[32,16,1024]{2,1,0:T(8,128)(2,1)S(1)}, u32[]{:S(2)}, u32[]{:S(2)}) async-start(bf16[32,16,1024]{2,1,0:T(8,128)(2,1)} %bitcast.3), calls=%async_computation.1 | async-start | bytes 2097152 | tf_op jit(solution)/shard_map/all_to_all | solution.py:35
  36.0 135.3 %all-gather.3.cloned.1.call-start = ((), (), s32[]{:S(2)}) async-start(), calls=%async_computation.2 | async-start | bytes 2703360 | tf_op jit(solution)/shard_map/all_gather | solution.py:54
  54.3 298.9 %all-reduce.3.cloned.1.call-start = ((), (), s32[]{:S(2)}) async-start(), calls=%async_computation.4 | async-start | bytes 2097152 | tf_op jit(solution)/shard_map/psum | solution.py:58
  98.8 76.2 %copy-start.1 = (bf16[1280,1024]{1,0:T(8,128)(2,1)S(1)}, bf16[1280,1024]{1,0:T(8,128)(2,1)}, u32[]{:S(2)}) copy-start(bf16[1280,1024]{1,0:T(8,128)(2,1)} %all-gather.5.cloned.1.call-done) | copy-start | bytes 7864324
Sparse Core Ops, SparseCore 0:
  10.7 85.4 all-gather.4
  98.9 72.3 all-gather.2
  179.5 173.6 all-reduce.2
where the time goes:
time: 366 us; the launch traced here: 363 us
  waiting for transfers between devices  310 us (85%)
  starting transfers between devices  14.6 us (4%)
  between operations  13.8 us (4%)
  matrix products  11.6 us (3%)
  local copies, waits for them, and re-layouts  8.97 us (2%)
    psum x1, waiting for transfers between devices, on_device(): total_up, total_down = lax.psum((partial_up, partial_down), 'owner')  174 us
    all_gather x1, waiting for transfers between devices, on_device(): lax.all_gather(ngram_grad, 'dp', axis=0, tiled=True)  72.5 us
    all_gather x1, waiting for transfers between devices, on_device(): lax.all_gather(ngram_input, 'dp', axis=0, tiled=True)  41.8 us
    all_to_all x1, waiting for transfers between devices, on_device(): lax.all_to_all(send_rows.reshape(owners, capacity, width), 'owner', split...  16 us
    all_to_all x1, starting transfers between devices, on_device(): lax.all_to_all(send_slots.reshape(owners, capacity), 'owner', split_axis=...  10.5 us
  transfers between devices with their start and end apart: 5, of which 5 were waited for; matrix products, arithmetic and copies ran while one was open for 3% of the time, Pallas kernels for 0%

commit v1 on v0

v1 whole, which is shorter than its diff:
```python
import functools

import jax
import jax.numpy as jnp
from jax import lax
from jax.experimental import pallas as pl
from jax.experimental.pallas import tpu as pltpu
from jax.sharding import PartitionSpec as P

MESH = pl.DeviceIdType.MESH
BF = jnp.bfloat16
F32 = jnp.float32
I32 = jnp.int32
NN = (((1,), (0,)), ((), ()))
NT = (((1,), (1,)), ((), ()))


def dot(a, b, dims):
    return lax.dot_general(a, b, dims, preferred_element_type=F32)


def one_hot(mask):
    return jnp.where(mask, 1.0, 0.0).astype(BF)


def flip(a):
    n = a.shape[1]
    eye = one_hot(lax.broadcasted_iota(I32, (n, n), 0) == lax.broadcasted_iota(I32, (n, n), 1))
    return dot(eye, a, NT).astype(BF)


def kernel(
    cfg, rows_ref, owner_ref, slot_ref, xin_ref, up_ref, down_ref, gu_ref, gd_ref,
    gt, codes, rbuf, acc, obuf, a2buf, ubuf, sibx, xs, gs, act, dgelu, pt, cx, full, s1, cy,
    a1_send, a1_recv, c1_send, c1_recv, sx_send, sx_recv, ring_send, ring_recv, sib_send, sib_recv,
    a2_send, a2_recv, cx_send, cx_recv, cy_send, cy_recv,
):
    nx, ny, nz = cfg
    owners = nx * ny
    tok, width = rows_ref.shape
    ng = xin_ref.shape[0]
    hid = up_ref.shape[1]
    share = width // owners
    half = width // 2
    sub = half // 2
    steps = nz // 2
    pair = 2 * ng
    sect = half // share
    tens = ng // 4
    low = (owners // 2) * 16

    dp, ow = lax.axis_index("dp"), lax.axis_index("owner")
    z, c = dp // 2, dp % 2
    px, py = ow // ny, ow % ny
    sibling = (z * 2 + (1 - c), ow)
    onward = (lax.rem(z + 1, nz) * 2 + c, ow)
    back = (lax.rem(z + nz - 1, nz) * 2 + c, ow)

    def remote(src, dst, send, recv, device):
        return pltpu.make_async_remote_copy(
            src_ref=src, dst_ref=dst, send_sem=send, recv_sem=recv, device_id=device, device_id_type=MESH
        )

    def arrived(dst, send, recv):
        remote(dst, dst, send, recv, sibling).wait_recv()

    def gone(src, send, recv):
        remote(src, src, send, recv, sibling).wait_send()

    def nth(t):
        off = jnp.where(t % 2 == 1, (t + 1) // 2, owners - t // 2)
        return lax.rem(ow + off, owners)

    barrier = pltpu.get_barrier_semaphore()

    def greet(device):
        pl.semaphore_signal(barrier, inc=1, device_id=device, device_id_type=MESH)

    def greet_plane(t, _):
        greet((z * 2, nth(t)))
        greet((z * 2 + 1, nth(t)))
        return 0

    lax.fori_loop(1, owners, greet_plane, 0)
    greet(sibling)
    greet(onward)
    greet(back)

    for b in range(width // 256 if width >= 256 else 1):
        w = min(width, 256)
        gt[b * w:(b + 1) * w, :] = flip(rows_ref[:, b * w:(b + 1) * w])
    owner, slot = owner_ref[...], slot_ref[...]
    k = (
        (slot >= tens).astype(I32) + (slot >= 2 * tens).astype(I32) + (slot >= 3 * tens).astype(I32)
    )
    lo = (owner // 2) * 16 + slot - tens * k
    hi = (owner % 2) * 4 + k
    codes[ow] = hi * 1024 + lo

    pl.semaphore_wait(barrier, 2 * (owners - 1) + 3)

    def half_of(ref, which):
        return ref.at[:, pl.ds(pl.multiple_of(which * half, half), half)]

    swap = remote(half_of(xin_ref, 1 - c), sibx, sx_send, sx_recv, sibling)
    swap.start()

    def rows_to(j):
        return remote(
            gt.at[pl.ds(pl.multiple_of(j * share, share), share)], rbuf.at[ow],
            a1_send.at[j], a1_recv.at[ow], (dp, j),
        )

    def codes_to(j):
        return remote(codes.at[ow], codes.at[ow], c1_send.at[j], c1_recv.at[ow], (dp, j))

    def send_rows(t, _):
        j = nth(t)
        codes_to(j).start()
        rows_to(j).start()
        return 0

    lax.fori_loop(1, owners, send_rows, 0)
    rbuf[ow] = gt[pl.ds(pl.multiple_of(ow * share, share), share), :]

    def piece(buf, block, core, h):
        return buf.at[
            pl.ds(pl.multiple_of(block * pair, 16), pair),
            pl.ds(pl.multiple_of(core * half + h * sub, sub), sub),
        ]

    def to_sibling(n, buf, block, h):
        ref = piece(buf, block, c, h)
        return remote(ref, ref, sib_send.at[n, block, h], sib_recv.at[n, block, h], sibling)

    def to_ring(n, buf, block, d, s, h):
        ref = piece(buf, block, c, h)
        return remote(
            ref, ref, ring_send.at[n, d, s, h], ring_recv.at[n, d, s, h], back if d else onward
        )

    def ring_start(n, buf):
        for h in (0, 1):
            for d in (0, 1):
                to_ring(n, buf, z, d, 0, h).start()
        for h in (0, 1):
            to_sibling(n, buf, z, h).start()

    def ring_step(n, buf, s):
        for h in (0, 1):
            for d in (0, 1):
                block = lax.rem(z + s + 1, nz) if d else lax.rem(z + nz - s - 1, nz)
                last = steps - 1 if h == d else steps - 2

                @pl.when(s <= last)
                def _():
                    arrived(piece(buf, block, c, h), ring_send.at[n, d, s, h], ring_recv.at[n, d, s, h])

                    @pl.when(s < last)
                    def _():
                        to_ring(n, buf, block, d, s + 1, h).start()

                    to_sibling(n, buf, block, h).start()

    def sibling_all(n, buf):
        def one(block, _):
            for h in (0, 1):
                arrived(piece(buf, block, 1 - c, h), sib_send.at[n, block, h], sib_recv.at[n, block, h])
            return 0

        lax.fori_loop(0, nz, one, 0)

    def ring_drain(n, buf):
        def one(s, _):
            for h in (0, 1):
                for d in (0, 1):
                    last = steps - 1 if h == d else steps - 2

                    @pl.when(s <= last)
                    def _():
                        gone(piece(buf, z, c, h), ring_send.at[n, d, s, h], ring_recv.at[n, d, s, h])

            return 0

        lax.fori_loop(0, steps, one, 0)

        def two(block, _):
            for h in (0, 1):
                gone(piece(buf, block, c, h), sib_send.at[n, block, h], sib_recv.at[n, block, h])
            return 0

        lax.fori_loop(0, nz, two, 0)

    def put_own(buf, value):
        here = pl.ds(pl.multiple_of(z * pair, 16), pair)
        for core in (0, 1):

            @pl.when(c == core)
            def _():
                buf[here, core * half:(core + 1) * half] = value

    swap.wait_recv()
    for core in (0, 1):

        @pl.when(c == core)
        def _():
            mine = xin_ref[:, core * half:(core + 1) * half].astype(F32)
            other = sibx[...].astype(F32)
            both = (mine, other) if core == 0 else (other, mine)
            xs[pl.ds(pl.multiple_of(z * pair, 16), pair), core * half:(core + 1) * half] = (
                jnp.concatenate(both, axis=0).astype(BF)
            )

    ring_start(0, xs)

    row_low = lax.broadcasted_iota(I32, (low, tok), 0)
    row_high = lax.broadcasted_iota(I32, (8 * share, tok), 0) // share
    acc[...] = jnp.zeros_like(acc)

    def sum_four(g, _):
        for q in range(4):
            t = 4 * g + q
            src = nth(t)

            @pl.when(t > 0)
            def _():
                arrived(codes.at[src], c1_send.at[src], c1_recv.at[src])
                arrived(rbuf.at[src], a1_send.at[src], a1_recv.at[src])

        total = acc[...]
        for q in range(4):
            src = nth(4 * g + q)
            code = codes[src]
            rows = rbuf[src]
            left = one_hot(row_low == code % 1024)
            right = jnp.concatenate([rows] * 8, axis=0) * one_hot(row_high == code // 1024)
            total = total + dot(left, right, NT)
        acc[...] = total
        ring_step(0, xs, g)
        return 0

    lax.fori_loop(0, steps, sum_four, 0)
    obuf[...] = acc[...].astype(BF)

    home = ow // sect
    seat = ow % sect

    def seat_of(core, s):
        return a2buf.at[
            pl.ds(pl.multiple_of((core * (sect // 4) + s // 4) * 16, 16), 16),
            pl.ds(pl.multiple_of((s % 4) * 128, 128), 128),
        ]

    def sums_of(o):
        return obuf.at[
            pl.ds(pl.multiple_of((o // 2) * 16, 16), 16), pl.ds(pl.multiple_of((o % 2) * 128, 128), 128)
        ]

    def sums_to(o):
        return remote(
            sums_of(o), seat_of(c, seat), a2_send.at[o], a2_recv.at[c * sect + seat], (z * 2 + home, o)
        )

    at_home = home == c

    def send_sums(t, _):
        sums_to(nth(t)).start()
        return 0

    lax.fori_loop(1, owners, send_sums, 0)

    @pl.when(at_home)
    def _():
        keep = pltpu.make_async_copy(sums_of(ow), seat_of(c, seat), a2_send.at[ow])
        keep.start()
        keep.wait()

    @pl.when(jnp.logical_not(at_home))
    def _():
        sums_to(ow).start()

    a = lax.broadcasted_iota(I32, (512, 512), 0)
    b = lax.broadcasted_iota(I32, (512, 512), 1)
    order = one_hot(b == ((a // 32) % 4) * 128 + (a // 128) * 32 + a % 32)
    n = lax.broadcasted_iota(I32, (pair, 128), 0)
    core_of = (n >= ng).astype(I32)
    n = n - ng * core_of
    k = (n >= tens).astype(I32) + (n >= 2 * tens).astype(I32) + (n >= 3 * tens).astype(I32)
    pick = one_hot(
        lax.broadcasted_iota(I32, (pair, 128), 1) == core_of * 64 + k * 16 + n - tens * k
    )
    up_t = flip(up_ref[...])

    def take_sums(u, _):
        core, s = u // sect, u % sect

        @pl.when(jnp.logical_not(jnp.logical_and(core == c, c * sect + s == ow)))
        def _():
            arrived(seat_of(core, s), a2_send.at[0], a2_recv.at[u])

        return 0

    lax.fori_loop(0, owners, take_sums, 0)
    placed = dot(a2buf[...], order, NN).astype(BF)
    parts = sect // 4
    for core in (0, 1):
        for k in range(4):
            for part in range(parts):
                ubuf[(core * 4 + k) * 16:(core * 4 + k + 1) * 16, part * 128:(part + 1) * 128] = placed[
                    (core * parts + part) * 16:(core * parts + part + 1) * 16, k * 128:(k + 1) * 128
                ]
    put_own(gs, dot(pick, ubuf[...], NN).astype(BF))
    ring_start(1, gs)

    sibling_all(0, xs)
    pre = dot(up_t, xs[...], NT)
    scale = 0.7978845608028654
    t = jnp.tanh(scale * (pre + 0.044715 * (pre * pre * pre)))
    act[...] = (pre * (0.5 * (1.0 + t))).astype(BF)
    dgelu[...] = 0.5 * (1.0 + t) + (0.5 * pre) * (1.0 - t * t) * (
        scale * (1.0 + (3.0 * 0.044715) * (pre * pre))
    )

    def next_step(s, _):
        ring_step(1, gs, s)
        return 0

    lax.fori_loop(0, steps, next_step, 0)
    sibling_all(1, gs)

    band = width // nx

    def cx_to(w, xx):
        return remote(
            pt.at[w, pl.ds(pl.multiple_of(xx * band, band), band)], cx.at[w, px],
            cx_send.at[w, xx], cx_recv.at[w, px], (dp, xx * ny + py),
        )

    def cy_to(w, yy):
        return remote(
            s1.at[w, pl.ds(pl.multiple_of(yy * share, share), share)], cy.at[w, py],
            cy_send.at[w, yy], cy_recv.at[w, py], (dp, px * ny + yy),
        )

    def send_partial(w, value):
        step = min(width, 256)
        for b in range(width // step):
            pt[w, b * step:(b + 1) * step, :] = flip(value[:, b * step:(b + 1) * step].astype(BF))
        for i in range(1, nx):
            cx_to(w, lax.rem(px + i, nx)).start()

    def along_x(w):
        total = pt[w, pl.ds(pl.multiple_of(px * band, band), band), :].astype(F32)
        for i in range(1, nx):
            xx = lax.rem(px + i, nx)
            arrived(cx.at[w, xx], cx_send.at[w, xx], cx_recv.at[w, xx])
            total = total + cx[w, xx].astype(F32)
        full[w] = total
        s1[w] = total.astype(BF)
        for i in range(1, ny):
            cy_to(w, lax.rem(py + i, ny)).start()

    def along_y(w):
        total = full[w, pl.ds(pl.multiple_of(py * share, share), share), :]
        for i in range(1, ny):
            yy = lax.rem(py + i, ny)
            arrived(cy.at[w, yy], cy_send.at[w, yy], cy_recv.at[w, yy])
            total = total + cy[w, yy].astype(F32)
        return total

    d_act = dot(down_ref[...], gs[...], NT)
    send_partial(1, dot(act[...], gs[...], NN))
    d_pre = (d_act * dgelu[...]).astype(BF)
    send_partial(0, dot(d_pre, xs[...], NN))
    along_x(1)
    along_x(0)
    down = along_y(1)
    gu_ref[...] = along_y(0)
    wide = jnp.concatenate([down, jnp.zeros((hid - share, hid), F32)], axis=0)
    gd_ref[...] = wide.T[:, :share]

    def drain(t, _):
        j = nth(t)
        rows_to(j).wait_send()
        codes_to(j).wait_send()
        sums_to(j).wait_send()
        return 0

    lax.fori_loop(1, owners, drain, 0)

    @pl.when(jnp.logical_not(at_home))
    def _():
        sums_to(ow).wait_send()

    swap.wait_send()
    ring_drain(0, xs)
    ring_drain(1, gs)
    for w in (0, 1):
        for i in range(1, nx):
            cx_to(w, lax.rem(px + i, nx)).wait_send()
        for i in range(1, ny):
            cy_to(w, lax.rem(py + i, ny)).wait_send()


def on_device(cfg, grad_rows, token_owner, token_slot, ngram_input, up_weight, down_weight):
    nx, ny, nz = cfg
    owners = nx * ny
    tok, width = grad_rows.shape
    ng = ngram_input.shape[0]
    hid = up_weight.shape[1]
    share, half = width // owners, width // 2
    low = (owners // 2) * 16
    total = 2 * nz * ng
    sect = half // share
    dma = pltpu.SemaphoreType.DMA
    vm = pl.BlockSpec(memory_space=pltpu.VMEM)
    return pl.pallas_call(
        functools.partial(kernel, cfg),
        out_shape=(
            jax.ShapeDtypeStruct((share, hid), F32),
            jax.ShapeDtypeStruct((hid, share), F32),
        ),
        in_specs=[vm] * 6,
        out_specs=(vm, vm),
        scratch_shapes=[
            pltpu.VMEM((width, tok), BF),
            pltpu.VMEM((owners, 1, tok), I32),
            pltpu.VMEM((owners, share, tok), BF),
            pltpu.VMEM((low, 8 * share), F32),
            pltpu.VMEM((low, 8 * share), BF),
            pltpu.VMEM((sect // 2 * 16, 512), BF),
            pltpu.VMEM((128, half), BF),
            pltpu.VMEM((ng, half), BF),
            pltpu.VMEM((total, width), BF),
            pltpu.VMEM((total, width), BF),
            pltpu.VMEM((hid, total), BF),
            pltpu.VMEM((hid, total), F32),
            pltpu.VMEM((2, width, hid), BF),
            pltpu.VMEM((2, nx, width // nx, hid), BF),
            pltpu.VMEM((2, width // nx, hid), F32),
            pltpu.VMEM((2, width // nx, hid), BF),
            pltpu.VMEM((2, ny, share, hid), BF),
            dma((owners,)), dma((owners,)),
            dma((owners,)), dma((owners,)),
            dma, dma,
            dma((2, 2, nz // 2, 2)), dma((2, 2, nz // 2, 2)),
            dma((2, nz, 2)), dma((2, nz, 2)),
            dma((owners,)), dma((owners,)),
            dma((2, nx)), dma((2, nx)),
            dma((2, ny)), dma((2, ny)),
        ],
        compiler_params=pltpu.CompilerParams(
            collective_id=0, has_side_effects=True, vmem_limit_bytes=48 * 1024 * 1024
        ),
        name="ngram_backward",
    )(
        grad_rows, token_owner.reshape(1, tok), token_slot.reshape(1, tok),
        ngram_input, up_weight, down_weight,
    )


def solution(mesh):
    owners, dp = mesh.shape["owner"], mesh.shape["dp"]
    nx = 4 if owners == 32 else 2
    cfg = (nx, owners // nx, dp // 2)
    in_specs = (
        P(("dp", "owner"), None),
        P(("dp", "owner")),
        P(("dp", "owner")),
        P(("dp", "owner"), None),
        P(None, "dp"),
        P("dp", None),
    )
    out_specs = (P("owner", "dp"), P("dp", "owner"))
    return jax.shard_map(
        functools.partial(on_device, cfg), mesh=mesh, in_specs=in_specs, out_specs=out_specs, check_vma=False
    )
```

time: 366 us -> 117 us (0.32)
  waiting for transfers between devices: 310 us -> 0 us
  Pallas kernels: 0 us -> 110 us
  starting transfers between devices: 14.6 us -> 0 us
  between operations: 13.8 us -> 0.66 us
  matrix products: 11.6 us -> 0 us
    psum x1 -> x0, waiting for transfers between devices: 174 us -> none  [on_device(): total_up, total_down = lax.psum((partial_up, partial_down), 'owner')]
    all_gather x2 -> x0, waiting for transfers between devices: 114 us -> none  [the longest x1 72.5 us: on_device(): lax.all_gather(ngram_grad, 'dp', axis=0, tiled=True)]
    pallas_call x0 -> x1, Pallas kernels: none -> 110 us  [on_device(): pl.pallas_call(functools.partial(kernel, cfg), out_shape=(jax.ShapeDtypeS...]
    all_to_all x2 -> x0, waiting for transfers between devices: 21.4 us -> none  [the longest x1 16 us: on_device(): lax.all_to_all(send_rows.reshape(owners, capacity, width), 'owner', split...]
    all_to_all x2 -> x0, starting transfers between devices: 14.4 us -> none  [the longest x1 10.5 us: on_device(): lax.all_to_all(send_slots.reshape(owners, capacity), 'owner', split_axis=...]
    dot_general x4 -> x0, matrix products: 11.6 us -> none  [the longest x1 4.42 us: block_terms(): lax.dot_general(inputs, d_pre, (((0,), (0,)), ((), ())), preferred_elemen...]
    scatter x2 -> x0, local copies, waits for them, and re-layouts: 4.56 us -> none  [the longest x1 3.17 us: on_device(): jnp.zeros((owners * capacity, width), jnp.bfloat16).at[placing]]
    unnamed x5 -> x13, local copies, waits for them, and re-layouts: 0.7 us -> 5.11 us
  transfers between devices with their start and end apart: 5 -> 0, of which waited for: 5 -> 0; matrix products, arithmetic and copies ran while one was open for 3% -> 0% of each run, Pallas kernels for 0% -> 0%
where the time goes in v1:
time: 117 us
  Pallas kernels  110 us (94%)
  local copies, waits for them, and re-layouts  5.79 us (5%)
    pallas_call x1, Pallas kernels, on_device(): pl.pallas_call(functools.partial(kernel, cfg), out_shape=(jax.ShapeDtypeS...  110 us
    unnamed x13, local copies, waits for them, and re-layouts  5.11 us

profile of v1, /device:TPU:1, one launch (start us, length us, event | category | flops | bytes accessed | tf_op | source)
XLA Modules:
  0.0 116.9 jit_solution(5806630231695326465)
XLA Ops:
  0.6 0.0 copy-start.5
  0.6 0.0 copy-start.4
  0.7 0.7 copy-done.5
  1.3 0.0 copy-done.4
  1.3 0.0 copy-start
  1.3 1.0 copy-done
  2.4 0.0 copy-start.1
  2.4 0.9 copy-done.1
  3.3 0.0 copy-start.2
  3.3 0.9 copy-done.2
  4.3 0.0 copy-start.3
  4.3 0.9 copy-done.3
  5.2 110.5 %ngram_backward.1 = (f32[32,128]{1,0:T(8,128)S(1)}, f32[128,32]{1,0:T(8,128)S(1)}) custom-call(bf16[256,1024]{1,0:T(8,128)(2,1)S(1)} %copy-done, s32[1,256]{1,0:T(1,128)S(1)} %bitcast.2, s32[1,256]{1,0:T(1,128)S(1)} %bitcast.3, bf16[40,1024]{1,0:T(8,128)(2,1)S(1)} %copy-done.3, bf16[1024,128]{1,0:T(8,128)(2,1)S(1)} %copy-done.1, bf16[128,1024]{1,0:T(8,128)(2,1)S(1)} %copy-done.2), custom_call_target="tpu_custom_call" | custom-call | tf_op jit(solution)/shard_map/ngram_backward/pallas_call | solution.py:417
  115.6 0.7 copy.8
  116.3 0.6 copy.10
Async XLA Ops:
  0.6 0.7 copy-start.5
  0.6 0.7 copy-start.4
  1.3 1.0 copy-start
  2.4 0.9 copy-start.1
  3.3 0.9 copy-start.2
  4.3 0.9 copy-start.3

commit v2 on v0

v2 whole, which is shorter than its diff:
```python
import functools

import jax
import jax.numpy as jnp
from jax import lax
from jax.experimental import pallas as pl
from jax.experimental.pallas import tpu as pltpu
from jax.sharding import PartitionSpec as P

MESH = pl.DeviceIdType.MESH
BF = jnp.bfloat16
F32 = jnp.float32
I32 = jnp.int32
NN = (((1,), (0,)), ((), ()))
NT = (((1,), (1,)), ((), ()))

PIECES = 4


def dot(a, b, dims):
    return lax.dot_general(a, b, dims, preferred_element_type=F32)


def one_hot(mask):
    return jnp.where(mask, 1.0, 0.0).astype(BF)


def flip(a):
    n = a.shape[1]
    eye = one_hot(lax.broadcasted_iota(I32, (n, n), 0) == lax.broadcasted_iota(I32, (n, n), 1))
    return dot(eye, a, NT).astype(BF)


def offsets(owners):
    out = [0]
    for k in range(1, owners // 2):
        out += [k, owners - k]
    return out + [owners // 2]


def kernel(
    cfg, rows_hbm, owner_hbm, slot_hbm, xin_hbm, up_hbm, down_hbm, gu_ref, gd_ref,
    rows_ref, owner_ref, slot_ref, xin_ref, up_ref, down_ref,
    gt, codes, rbuf, acc, obuf, a2buf, ubuf, sums, sibx, sibg, xs, gs, act, dgelu, d_act, pt, cx, full, s1, cy,
    in_sem, a1_send, a1_recv, c1_send, c1_recv, sx_send, sx_recv, sg_send, sg_recv, ring_send, ring_recv, sib_send, sib_recv,
    a2_send, a2_recv, cx_send, cx_recv, cy_send, cy_recv,
):
    nx, ny, nz = cfg
    owners = nx * ny
    tok, width = rows_ref.shape
    ng = xin_ref.shape[0]
    share = width // owners
    half = width // 2
    sub = half // PIECES
    steps = nz // 2
    pair = 2 * ng
    tens = ng // 4
    low = (owners // 2) * 16
    offs = offsets(owners)
    groups = owners // 8

    dp, ow = lax.axis_index("dp"), lax.axis_index("owner")
    z, c = dp // 2, dp % 2
    sibling = (z * 2 + (1 - c), ow)

    def plane(t):
        return lax.rem(ow + offs[t], owners)

    def along(k):
        return (lax.rem(z + k + nz, nz) * 2 + c, ow)

    fetch = [
        pltpu.make_async_copy(a, b, in_sem.at[i])
        for i, (a, b) in enumerate((
            (rows_hbm, rows_ref), (owner_hbm, owner_ref), (slot_hbm, slot_ref),
            (xin_hbm, xin_ref), (up_hbm, up_ref), (down_hbm, down_ref),
        ))
    ]
    for copy in fetch:
        copy.start()

    barrier = pltpu.get_barrier_semaphore()

    def greet(device):
        pl.semaphore_signal(barrier, inc=1, device_id=device, device_id_type=MESH)

    greet(sibling)
    greet(along(1))
    greet(along(-1))
    for t in range(1, owners):
        greet((dp, plane(t)))

    def remote(src, dst, send, recv, device):
        return pltpu.make_async_remote_copy(
            src_ref=src, dst_ref=dst, send_sem=send, recv_sem=recv, device_id=device, device_id_type=MESH
        )

    def arrived(dst, recv):
        remote(dst, dst, recv, recv, sibling).wait_recv()

    def gone(src, send):
        remote(src, src, send, send, sibling).wait_send()

    fetch[1].wait()
    fetch[2].wait()
    owner, slot = owner_ref[...], slot_ref[...]
    k = (
        (slot >= tens).astype(I32) + (slot >= 2 * tens).astype(I32) + (slot >= 3 * tens).astype(I32)
    )
    lo = (owner >> 1) * 16 + slot - tens * k
    hi = (owner & 1) * 4 + k
    codes[0] = hi * 1024 + lo
    fetch[0].wait()
    wide = min(width, 256)
    for b in range(width // wide):
        gt[b * wide:(b + 1) * wide, :] = flip(rows_ref[:, b * wide:(b + 1) * wide])
    fetch[3].wait()

    pl.semaphore_wait(barrier, owners + 2)

    def swap_of(ref, other, send, recv):
        return remote(
            ref.at[:, pl.ds(pl.multiple_of((1 - c) * half, half), half)], other, send, recv, sibling
        )

    swap = swap_of(xin_ref, sibx, sx_send, sx_recv)
    swap.start()
    for t in range(1, owners):
        j = plane(t)
        remote(codes.at[0], codes.at[t], c1_send, c1_recv, (dp, j)).start()
        remote(
            gt.at[pl.ds(pl.multiple_of(j * share, share), share)], rbuf.at[t],
            a1_send, a1_recv.at[t // 8], (dp, j),
        ).start()
    rbuf[0] = gt[pl.ds(pl.multiple_of(ow * share, share), share), :]

    def spot(d, dist):
        return 0 if dist == 0 else 2 * steps - 1 if dist == steps else 2 * dist - 1 + d

    def piece(buf, at, h):
        return buf.at[
            pl.ds(at * pair, pair), pl.ds(pl.multiple_of(c * half + h * sub, sub), sub)
        ]

    def stretch(buf, at, first, count):
        return buf.at[
            pl.ds(at * pair, pair), pl.ds(pl.multiple_of(c * half + first * sub, sub), count * sub)
        ]

    def pieces_of(d, dist):
        return range(PIECES) if dist < steps else range(d * PIECES // 2, (d + 1) * PIECES // 2)

    def forward(n, buf, d, dist, h):
        if dist < steps and h in pieces_of(d, dist + 1):
            remote(
                piece(buf, spot(d, dist), h), piece(buf, spot(d, dist + 1), h),
                ring_send.at[n], ring_recv.at[n, d, dist, h], along(-1 if d else 1),
            ).start()

    def share_core(n, buf, d, dist):
        hs = pieces_of(d, dist)
        ref = stretch(buf, spot(d, dist), hs[0], len(hs))
        part = spot(d, dist) // steps
        remote(ref, ref, sib_send.at[n], sib_recv.at[n, part], sibling).start()

    def ring_start(n, buf):
        for h in range(PIECES):
            for d in (0, 1):
                forward(n, buf, d, 0, h)
        share_core(n, buf, 0, 0)

    def ring_step(n, buf, dist):
        for h in range(PIECES):
            for d in (0, 1):
                if h in pieces_of(d, dist):
                    arrived(piece(buf, spot(d, dist), h), ring_recv.at[n, d, dist - 1, h])
                    forward(n, buf, d, dist, h)
        for d in (0, 1):
            share_core(n, buf, d, dist)

    def sibling_part(n, buf, part):
        arrived(buf.at[pl.ds(part * steps * pair, steps * pair), pl.ds(0, half)], sib_recv.at[n, part])

    def ring_drain(n, buf):
        gone(buf.at[pl.ds(0, (2 * steps - 1) * pair), pl.ds(0, half)], ring_send.at[n])
        gone(buf.at[:, pl.ds(0, half)], sib_send.at[n])

    def put_own(buf, ref, other):
        for core in (0, 1):

            @pl.when(c == core)
            def _():
                both = [ref[:, core * half:(core + 1) * half].astype(F32), other[...].astype(F32)]
                both = both if core == 0 else both[::-1]
                buf[0:pair, core * half:(core + 1) * half] = jnp.concatenate(both, axis=0).astype(BF)

    swap.wait_recv()
    put_own(xs, xin_ref, sibx)
    ring_start(0, xs)

    a = lax.broadcasted_iota(I32, (512, 512), 0)
    b = lax.broadcasted_iota(I32, (512, 512), 1)
    order = one_hot(b == ((a >> 5) & 3) * 128 + (a >> 7) * 32 + (a & 31))
    n = lax.broadcasted_iota(I32, (ng, 64), 0)
    k = (n >= tens).astype(I32) + (n >= 2 * tens).astype(I32) + (n >= 3 * tens).astype(I32)
    pick = one_hot(lax.broadcasted_iota(I32, (ng, 64), 1) == k * 16 + n - tens * k)

    row_low = lax.broadcasted_iota(I32, (low, tok), 0).astype(BF)
    row_high = (lax.broadcasted_iota(I32, (8 * share, tok), 0) >> (share.bit_length() - 1)).astype(BF)
    one, zero = jnp.ones((), BF), jnp.zeros((), BF)
    acc[...] = jnp.zeros_like(acc)

    def sum_two(i, _):
        total = acc[...]
        for q in (0, 1):
            code = codes[2 * i + q]
            rows = rbuf[2 * i + q]
            left = jnp.where(row_low == (code & 1023).astype(F32).astype(BF), one, zero)
            right = jnp.where(
                row_high == (code >> 10).astype(F32).astype(BF), jnp.concatenate([rows] * 8, axis=0), zero
            )
            total = total + dot(left, right, NT)
        acc[...] = total
        return 0

    todo = list(range(1, steps + 1))

    def inputs_on(count):
        for _ in range(min(count, len(todo))):
            ring_step(0, xs, todo.pop(0))

    inputs_on(3)
    arrived(codes.at[pl.ds(1, owners - 1)], c1_recv)
    for g in range(groups):
        first = 1 if g == 0 else 0
        arrived(rbuf.at[pl.ds(8 * g + first, 8 - first)], a1_recv.at[g])
        lax.fori_loop(4 * g, 4 * g + 4, sum_two, 0)
        if g == 0:
            inputs_on(1)
    obuf[...] = acc[...].astype(BF)

    place = a2buf.at[
        pl.ds(pl.multiple_of((ow // 4) * 16, 16), 16), pl.ds(pl.multiple_of((ow % 4) * 128, 128), 128)
    ]

    def sums_of(o):
        return obuf.at[
            pl.ds(pl.multiple_of((o // 2) * 16, 16), 16), pl.ds(pl.multiple_of((o % 2) * 128, 128), 128)
        ]

    for t in range(1, owners):
        o = plane(t)
        remote(sums_of(o), place, a2_send, a2_recv, (dp, o)).start()
    pltpu.make_async_copy(sums_of(ow), place, a2_recv).start()
    fetch[4].wait()
    fetch[5].wait()
    up_t = flip(up_ref[...])
    inputs_on(2)
    arrived(a2buf, a2_recv)
    placed = dot(a2buf[...], order, NN).astype(BF)
    for k in range(4):
        for part in range(owners // 4):
            ubuf[k * 16:(k + 1) * 16, part * 128:(part + 1) * 128] = placed[
                part * 16:(part + 1) * 16, k * 128:(k + 1) * 128
            ]
    sums[...] = dot(pick, ubuf[...], NN).astype(BF)
    swap_sums = swap_of(sums, sibg, sg_send, sg_recv)
    swap_sums.start()
    swap_sums.wait_recv()
    put_own(gs, sums, sibg)
    ring_start(1, gs)

    chunk = xs.shape[0] // 2

    def hidden(i):
        at = slice(i * chunk, (i + 1) * chunk)
        pre = dot(up_t, xs[at, :], NT)
        scale = 0.7978845608028654
        t = jnp.tanh(scale * (pre + 0.044715 * (pre * pre * pre)))
        act[:, at] = (pre * (0.5 * (1.0 + t))).astype(BF)
        dgelu[:, at] = 0.5 * (1.0 + t) + (0.5 * pre) * (1.0 - t * t) * (
            scale * (1.0 + (3.0 * 0.044715) * (pre * pre))
        )

    def grads(i):
        at = slice(i * chunk, (i + 1) * chunk)
        d_act[:, at] = dot(down_ref[...], gs[at, :], NT)

    for dist in range(1, steps + 1):
        inputs_on(1)
        ring_step(1, gs, dist)
        if not todo:
            if dist >= steps // 2 and dist < steps // 2 + 2:
                i = dist - steps // 2
                sibling_part(0, xs, i)
                hidden(i)
            if dist == steps - 1:
                sibling_part(1, gs, 0)
                grads(0)
    sibling_part(1, gs, 1)

    band = width // nx
    px, py = ow // ny, ow % ny

    def send_partial(w, value):
        for b in range(width // wide):
            pt[w, b * wide:(b + 1) * wide, :] = flip(value[:, b * wide:(b + 1) * wide].astype(BF))
        for i in range(1, nx):
            xx = lax.rem(px + i, nx)
            remote(
                pt.at[w, pl.ds(pl.multiple_of(xx * band, band), band)], cx.at[w, i - 1],
                cx_send.at[w], cx_recv.at[w], (dp, xx * ny + py),
            ).start()

    def along_x(w):
        arrived(cx.at[w], cx_recv.at[w])
        total = pt[w, pl.ds(pl.multiple_of(px * band, band), band), :].astype(F32)
        for i in range(1, nx):
            total = total + cx[w, i - 1].astype(F32)
        full[w] = total
        s1[w] = total.astype(BF)
        for i in range(1, ny):
            yy = lax.rem(py + i, ny)
            remote(
                s1.at[w, pl.ds(pl.multiple_of(yy * share, share), share)], cy.at[w, i - 1],
                cy_send.at[w], cy_recv.at[w], (dp, px * ny + yy),
            ).start()

    def along_y(w):
        arrived(cy.at[w], cy_recv.at[w])
        total = full[w, pl.ds(pl.multiple_of(py * share, share), share), :]
        for i in range(1, ny):
            total = total + cy[w, i - 1].astype(F32)
        return total

    send_partial(1, dot(act[...], gs[...], NN))
    grads(1)
    send_partial(0, dot((d_act[...] * dgelu[...]).astype(BF), xs[...], NN))
    along_x(1)
    along_x(0)
    gd_ref[...] = along_y(1)
    gu_ref[...] = along_y(0)

    gone(codes.at[pl.ds(1, owners - 1)], c1_send)
    gone(gt.at[pl.ds(0, (owners - 1) * share)], a1_send)
    gone(gt.at[pl.ds(0, (owners - 1) * 16), pl.ds(0, 128)], a2_send)

    swap.wait_send()
    swap_sums.wait_send()
    ring_drain(0, xs)
    ring_drain(1, gs)
    for w in (0, 1):
        gone(cx.at[w], cx_send.at[w])
        gone(cy.at[w], cy_send.at[w])


def on_device(cfg, grad_rows, token_owner, token_slot, ngram_input, up_weight, down_weight):
    nx, ny, nz = cfg
    owners = nx * ny
    tok, width = grad_rows.shape
    ng = ngram_input.shape[0]
    hid = up_weight.shape[1]
    share, half = width // owners, width // 2
    low = (owners // 2) * 16
    total = 2 * nz * ng
    dma = pltpu.SemaphoreType.DMA
    vm = pl.BlockSpec(memory_space=pltpu.VMEM)
    far = pl.BlockSpec(memory_space=pltpu.HBM)
    up, down = pl.pallas_call(
        functools.partial(kernel, cfg),
        out_shape=(
            jax.ShapeDtypeStruct((share, hid), F32),
            jax.ShapeDtypeStruct((share, hid), F32),
        ),
        in_specs=[far] * 6,
        out_specs=(vm, vm),
        scratch_shapes=[
            pltpu.VMEM((tok, width), BF),
            pltpu.VMEM((1, tok), I32),
            pltpu.VMEM((1, tok), I32),
            pltpu.VMEM((ng, width), BF),
            pltpu.VMEM((width, hid), BF),
            pltpu.VMEM((hid, width), BF),
            pltpu.VMEM((width, tok), BF),
            pltpu.VMEM((owners, 1, tok), I32),
            pltpu.VMEM((owners, share, tok), BF),
            pltpu.VMEM((low, 8 * share), F32),
            pltpu.VMEM((low, 8 * share), BF),
            pltpu.VMEM((owners // 4 * 16, 512), BF),
            pltpu.VMEM((64, width), BF),
            pltpu.VMEM((ng, width), BF),
            pltpu.VMEM((ng, half), BF),
            pltpu.VMEM((ng, half), BF),
            pltpu.VMEM((total, width), BF),
            pltpu.VMEM((total, width), BF),
            pltpu.VMEM((hid, total), BF),
            pltpu.VMEM((hid, total), F32),
            pltpu.VMEM((hid, total), F32),
            pltpu.VMEM((2, width, hid), BF),
            pltpu.VMEM((2, nx - 1, width // nx, hid), BF),
            pltpu.VMEM((2, width // nx, hid), F32),
            pltpu.VMEM((2, width // nx, hid), BF),
            pltpu.VMEM((2, ny - 1, share, hid), BF),
            dma((6,)),
            dma, dma((owners // 8,)),
            dma, dma,
            dma, dma, dma, dma,
            dma((2,)), dma((2, 2, nz // 2, PIECES)),
            dma((2,)), dma((2, 2)),
            dma, dma,
            dma((2,)), dma((2,)),
            dma((2,)), dma((2,)),
        ],
        compiler_params=pltpu.CompilerParams(
            collective_id=0, has_side_effects=True, vmem_limit_bytes=56 * 1024 * 1024
        ),
        name="ngram_backward",
    )(
        grad_rows, token_owner.reshape(1, tok), token_slot.reshape(1, tok),
        ngram_input, up_weight, down_weight,
    )
    return up, down.T


def solution(mesh):
    owners, dp = mesh.shape["owner"], mesh.shape["dp"]
    nx = 4 if owners == 32 else 2
    cfg = (nx, owners // nx, dp // 2)
    in_specs = (
        P(("dp", "owner"), None),
        P(("dp", "owner")),
        P(("dp", "owner")),
        P(("dp", "owner"), None),
        P(None, "dp"),
        P("dp", None),
    )
    out_specs = (P("owner", "dp"), P("dp", "owner"))
    return jax.shard_map(
        functools.partial(on_device, cfg), mesh=mesh, in_specs=in_specs, out_specs=out_specs, check_vma=False
    )
```

time: 366 us -> 95.1 us (0.26)
  waiting for transfers between devices: 310 us -> 0 us
  Pallas kernels: 0 us -> 92.3 us
  starting transfers between devices: 14.6 us -> 0 us
  between operations: 13.8 us -> 0.65 us
  matrix products: 11.6 us -> 0 us
  local copies, waits for them, and re-layouts: 8.97 us -> 1.94 us
    psum x1 -> x0, waiting for transfers between devices: 174 us -> none  [on_device(): total_up, total_down = lax.psum((partial_up, partial_down), 'owner')]
    all_gather x2 -> x0, waiting for transfers between devices: 114 us -> none  [the longest x1 72.5 us: on_device(): lax.all_gather(ngram_grad, 'dp', axis=0, tiled=True)]
    pallas_call x0 -> x1, Pallas kernels: none -> 92.3 us  [on_device(): pl.pallas_call(functools.partial(kernel, cfg), out_shape=(jax.ShapeDtypeS...]
    all_to_all x2 -> x0, waiting for transfers between devices: 21.4 us -> none  [the longest x1 16 us: on_device(): lax.all_to_all(send_rows.reshape(owners, capacity, width), 'owner', split...]
    all_to_all x2 -> x0, starting transfers between devices: 14.4 us -> none  [the longest x1 10.5 us: on_device(): lax.all_to_all(send_slots.reshape(owners, capacity), 'owner', split_axis=...]
    dot_general x4 -> x0, matrix products: 11.6 us -> none  [the longest x1 4.42 us: block_terms(): lax.dot_general(inputs, d_pre, (((0,), (0,)), ((), ())), preferred_elemen...]
    scatter x2 -> x0, local copies, waits for them, and re-layouts: 4.56 us -> none  [the longest x1 3.17 us: on_device(): jnp.zeros((owners * capacity, width), jnp.bfloat16).at[placing]]
  transfers between devices with their start and end apart: 5 -> 0, of which waited for: 5 -> 0; matrix products, arithmetic and copies ran while one was open for 3% -> 0% of each run, Pallas kernels for 0% -> 0%
where the time goes in v2:
time: 95.1 us; the launch traced here: 94.9 us
  Pallas kernels  92.3 us (97%)
  local copies, waits for them, and re-layouts  1.94 us (2%)
    pallas_call x1, Pallas kernels, on_device(): pl.pallas_call(functools.partial(kernel, cfg), out_shape=(jax.ShapeDtypeS...  92.3 us
    unnamed x4, local copies, waits for them, and re-layouts  1.94 us

profile of v2, /device:TPU:1, one launch (start us, length us, event | category | flops | bytes accessed | tf_op | source)
XLA Modules:
  0.0 94.9 jit_solution(10541032066848959416)
XLA Ops:
  0.6 92.3 %ngram_backward.1 = (f32[32,128]{1,0:T(8,128)}, f32[32,128]{1,0:T(8,128)}) custom-call(bf16[256,1024]{1,0:T(8,128)(2,1)} %rows_hbm.1, s32[1,256]{1,0:T(1,128)} %bitcast.4, s32[1,256]{1,0:T(1,128)} %bitcast.5, bf16[40,1024]{1,0:T(8,128)(2,1)} %xin_hbm.1, bf16[1024,128]{1,0:T(8,128)(2,1)} %up_hbm.1, bf16[128,1024]{1,0:T(8,128)(2,1)} %down_hbm.1), custom_call_target="tpu_custom_call" | custom-call | tf_op jit(solution)/shard_map/ngram_backward/pallas_call | solution.py:369
  92.9 0.0 copy-start
  92.9 1.3 %copy.10 = f32[32,128]{1,0:T(8,128)} copy(f32[32,128]{1,0:T(8,128)} %get-tuple-element.8) | data formatting | bytes 32768
  94.3 0.0 copy-done
  94.3 0.6 copy.11
Async XLA Ops:
  92.9 1.3 %copy-start = (f32[32,128]{1,0:T(8,128)S(1)}, f32[32,128]{1,0:T(8,128)}, u32[]{:S(2)}) copy-start(f32[32,128]{1,0:T(8,128)} %get-tuple-element.5) | copy-start | bytes 49156

commit v3 on v2

--- a/solution.py
+++ b/solution.py
@@ -51,7 +51,7 @@
     ng = xin_ref.shape[0]
     share = width // owners
     half = width // 2
-    sub = half // PIECES
+    sub = width // PIECES
     steps = nz // 2
     pair = 2 * ng
     tens = ng // 4
@@ -118,12 +118,7 @@
 
     pl.semaphore_wait(barrier, owners + 2)
 
-    def swap_of(ref, other, send, recv):
-        return remote(
-            ref.at[:, pl.ds(pl.multiple_of((1 - c) * half, half), half)], other, send, recv, sibling
-        )
-
-    swap = swap_of(xin_ref, sibx, sx_send, sx_recv)
+    swap = remote(xin_ref, sibx, sx_send, sx_recv, sibling)
     swap.start()
     for t in range(1, owners):
         j = plane(t)
@@ -134,65 +129,59 @@
         ).start()
     rbuf[0] = gt[pl.ds(pl.multiple_of(ow * share, share), share), :]
 
-    def spot(d, dist):
-        return 0 if dist == 0 else 2 * steps - 1 if dist == steps else 2 * dist - 1 + d
-
-    def piece(buf, at, h):
-        return buf.at[
-            pl.ds(at * pair, pair), pl.ds(pl.multiple_of(c * half + h * sub, sub), sub)
-        ]
-
-    def stretch(buf, at, first, count):
-        return buf.at[
-            pl.ds(at * pair, pair), pl.ds(pl.multiple_of(c * half + first * sub, sub), count * sub)
-        ]
-
-    def pieces_of(d, dist):
-        return range(PIECES) if dist < steps else range(d * PIECES // 2, (d + 1) * PIECES // 2)
-
-    def forward(n, buf, d, dist, h):
-        if dist < steps and h in pieces_of(d, dist + 1):
+    onward = along(1 - 2 * c)
+
+    def rows_at(dist):
+        at = 0 if dist == 0 else 2 * steps - 1 if dist == steps else 2 * dist - 1 + c
+        return pl.ds(pl.multiple_of(at * pair, 16), pair)
+
+    def piece(buf, dist, h):
+        first = lax.rem(h * sub + c * half, width)
+        return buf.at[rows_at(dist), pl.ds(pl.multiple_of(first, sub), sub)]
+
+    def pieces_of(dist):
+        return range(PIECES if dist < steps else PIECES // 2)
+
+    def forward(n, buf, dist, h):
+        if dist < steps and h in pieces_of(dist + 1):
             remote(
-                piece(buf, spot(d, dist), h), piece(buf, spot(d, dist + 1), h),
-                ring_send.at[n], ring_recv.at[n, d, dist, h], along(-1 if d else 1),
+                piece(buf, dist, h), piece(buf, dist + 1, h),
+                ring_send.at[n], ring_recv.at[n, dist, h], onward,
             ).start()
-
-    def share_core(n, buf, d, dist):
-        hs = pieces_of(d, dist)
-        ref = stretch(buf, spot(d, dist), hs[0], len(hs))
-        part = spot(d, dist) // steps
-        remote(ref, ref, sib_send.at[n], sib_recv.at[n, part], sibling).start()
 
     def ring_start(n, buf):
         for h in range(PIECES):
-            for d in (0, 1):
-                forward(n, buf, d, 0, h)
-        share_core(n, buf, 0, 0)
+            forward(n, buf, 0, h)
 
     def ring_step(n, buf, dist):
-        for h in range(PIECES):
-            for d in (0, 1):
-                if h in pieces_of(d, dist):
-                    arrived(piece(buf, spot(d, dist), h), ring_recv.at[n, d, dist - 1, h])
-                    forward(n, buf, d, dist, h)
-        for d in (0, 1):
-            share_core(n, buf, d, dist)
+        for h in pieces_of(dist):
+            arrived(piece(buf, dist, h), ring_recv.at[n, dist - 1, h])
+            forward(n, buf, dist, h)
+        cols = pl.ds(0, width) if dist < steps else pl.ds(pl.multiple_of(c * half, half), half)
+        ref = buf.at[rows_at(dist), cols]
+        remote(
+            ref, ref, sib_send.at[n], sib_recv.at[n, 0 if dist <= steps // 2 else 1], sibling
+        ).start()
 
     def sibling_part(n, buf, part):
-        arrived(buf.at[pl.ds(part * steps * pair, steps * pair), pl.ds(0, half)], sib_recv.at[n, part])
+        if part == 0:
+            arrived(buf.at[pl.ds(0, steps // 2 * pair)], sib_recv.at[n, 0])
+        else:
+            arrived(buf.at[pl.ds(0, (steps - 1) * pair), pl.ds(0, half)], sib_recv.at[n, 1])
 
     def ring_drain(n, buf):
-        gone(buf.at[pl.ds(0, (2 * steps - 1) * pair), pl.ds(0, half)], ring_send.at[n])
-        gone(buf.at[:, pl.ds(0, half)], sib_send.at[n])
+        sent = buf.at[pl.ds(0, (2 * steps - 1) * pair), pl.ds(0, half)]
+        gone(sent, ring_send.at[n])
+        gone(sent, sib_send.at[n])
 
     def put_own(buf, ref, other):
         for core in (0, 1):
 
             @pl.when(c == core)
             def _():
-                both = [ref[:, core * half:(core + 1) * half].astype(F32), other[...].astype(F32)]
+                both = [ref[...].astype(F32), other[...].astype(F32)]
                 both = both if core == 0 else both[::-1]
-                buf[0:pair, core * half:(core + 1) * half] = jnp.concatenate(both, axis=0).astype(BF)
+                buf[0:pair, :] = jnp.concatenate(both, axis=0).astype(BF)
 
     swap.wait_recv()
     put_own(xs, xin_ref, sibx)
@@ -208,20 +197,17 @@
     row_low = lax.broadcasted_iota(I32, (low, tok), 0).astype(BF)
     row_high = (lax.broadcasted_iota(I32, (8 * share, tok), 0) >> (share.bit_length() - 1)).astype(BF)
     one, zero = jnp.ones((), BF), jnp.zeros((), BF)
-    acc[...] = jnp.zeros_like(acc)
-
-    def sum_two(i, _):
-        total = acc[...]
-        for q in (0, 1):
-            code = codes[2 * i + q]
-            rows = rbuf[2 * i + q]
-            left = jnp.where(row_low == (code & 1023).astype(F32).astype(BF), one, zero)
-            right = jnp.where(
-                row_high == (code >> 10).astype(F32).astype(BF), jnp.concatenate([rows] * 8, axis=0), zero
-            )
-            total = total + dot(left, right, NT)
-        acc[...] = total
-        return 0
+
+    def sum_group(g):
+        left, right = [], []
+        for t in range(8 * g, 8 * g + 8):
+            code = codes[t]
+            left.append(jnp.where(row_low == (code & 1023).astype(F32).astype(BF), one, zero))
+            right.append(jnp.where(
+                row_high == (code >> 10).astype(F32).astype(BF), jnp.concatenate([rbuf[t]] * 8, axis=0), zero
+            ))
+        total = dot(jnp.concatenate(left, axis=1), jnp.concatenate(right, axis=1), NT)
+        acc[...] = total if g == 0 else acc[...] + total
 
     todo = list(range(1, steps + 1))
 
@@ -234,7 +220,7 @@
     for g in range(groups):
         first = 1 if g == 0 else 0
         arrived(rbuf.at[pl.ds(8 * g + first, 8 - first)], a1_recv.at[g])
-        lax.fori_loop(4 * g, 4 * g + 4, sum_two, 0)
+        sum_group(g)
         if g == 0:
             inputs_on(1)
     obuf[...] = acc[...].astype(BF)
@@ -264,7 +250,7 @@
                 part * 16:(part + 1) * 16, k * 128:(k + 1) * 128
             ]
     sums[...] = dot(pick, ubuf[...], NN).astype(BF)
-    swap_sums = swap_of(sums, sibg, sg_send, sg_recv)
+    swap_sums = remote(sums, sibg, sg_send, sg_recv, sibling)
     swap_sums.start()
     swap_sums.wait_recv()
     put_own(gs, sums, sibg)
@@ -389,8 +375,8 @@
             pltpu.VMEM((owners // 4 * 16, 512), BF),
             pltpu.VMEM((64, width), BF),
             pltpu.VMEM((ng, width), BF),
-            pltpu.VMEM((ng, half), BF),
-            pltpu.VMEM((ng, half), BF),
+            pltpu.VMEM((ng, width), BF),
+            pltpu.VMEM((ng, width), BF),
             pltpu.VMEM((total, width), BF),
             pltpu.VMEM((total, width), BF),
             pltpu.VMEM((hid, total), BF),
@@ -405,7 +391,7 @@
             dma, dma((owners // 8,)),
             dma, dma,
             dma, dma, dma, dma,
-            dma((2,)), dma((2, 2, nz // 2, PIECES)),
+            dma((2,)), dma((2, nz // 2, PIECES)),
             dma((2,)), dma((2, 2)),
             dma, dma,
             dma((2,)), dma((2,)),

time: 95.1 us -> 89.8 us (0.944)
  Pallas kernels: 92.3 us -> 87 us
    pallas_call x1, Pallas kernels: 92.3 us -> 87 us  [on_device(): pl.pallas_call(functools.partial(kernel, cfg), out_shape=(jax.ShapeDtypeS...]
where the time goes in v3:
time: 89.8 us; the launch traced here: 89.6 us
  Pallas kernels  87 us (97%)
  local copies, waits for them, and re-layouts  1.94 us (2%)
    pallas_call x1, Pallas kernels, on_device(): pl.pallas_call(functools.partial(kernel, cfg), out_shape=(jax.ShapeDtypeS...  87 us
    unnamed x4, local copies, waits for them, and re-layouts  1.94 us

profile of v3, /device:TPU:1, one launch (start us, length us, event | category | flops | bytes accessed | tf_op | source)
XLA Modules:
  0.0 89.6 jit_solution(10129007904435744671)
XLA Ops:
  0.6 87.0 %ngram_backward.1 = (f32[32,128]{1,0:T(8,128)}, f32[32,128]{1,0:T(8,128)}) custom-call(bf16[256,1024]{1,0:T(8,128)(2,1)} %rows_hbm.1, s32[1,256]{1,0:T(1,128)} %bitcast.4, s32[1,256]{1,0:T(1,128)} %bitcast.5, bf16[40,1024]{1,0:T(8,128)(2,1)} %xin_hbm.1, bf16[1024,128]{1,0:T(8,128)(2,1)} %up_hbm.1, bf16[128,1024]{1,0:T(8,128)(2,1)} %down_hbm.1), custom_call_target="tpu_custom_call" | custom-call | tf_op jit(solution)/shard_map/ngram_backward/pallas_call | solution.py:355
  87.6 0.0 copy-start
  87.6 1.3 %copy.10 = f32[32,128]{1,0:T(8,128)} copy(f32[32,128]{1,0:T(8,128)} %get-tuple-element.8) | data formatting | bytes 32768
  88.9 0.0 copy-done
  89.0 0.6 copy.11
Async XLA Ops:
  87.6 1.3 %copy-start = (f32[32,128]{1,0:T(8,128)S(1)}, f32[32,128]{1,0:T(8,128)}, u32[]{:S(2)}) copy-start(f32[32,128]{1,0:T(8,128)} %get-tuple-element.5) | copy-start | bytes 49156

commit v4 on v3

--- a/solution.py
+++ b/solution.py
@@ -31,11 +31,13 @@
     return dot(eye, a, NT).astype(BF)
 
 
-def offsets(owners):
-    out = [0]
-    for k in range(1, owners // 2):
-        out += [k, owners - k]
-    return out + [owners // 2]
+def offsets(nx, ny):
+    both = [(dx, dy) for dx in range(nx) for dy in range(ny)]
+    return sorted(both, key=lambda v: min(v[0], nx - v[0]) + min(v[1], ny - v[1]))
+
+
+def far_first(n):
+    return sorted(range(1, n), key=lambda i: -min(i, n - i))
 
 
 def kernel(
@@ -56,15 +58,17 @@
     pair = 2 * ng
     tens = ng // 4
     low = (owners // 2) * 16
-    offs = offsets(owners)
+    offs = offsets(nx, ny)
     groups = owners // 8
 
     dp, ow = lax.axis_index("dp"), lax.axis_index("owner")
     z, c = dp // 2, dp % 2
+    px, py = ow // ny, ow % ny
     sibling = (z * 2 + (1 - c), ow)
 
     def plane(t):
-        return lax.rem(ow + offs[t], owners)
+        dx, dy = offs[t]
+        return lax.rem(px + dx, nx) * ny + lax.rem(py + dy, ny)
 
     def along(k):
         return (lax.rem(z + k + nz, nz) * 2 + c, ow)
@@ -84,11 +88,11 @@
     def greet(device):
         pl.semaphore_signal(barrier, inc=1, device_id=device, device_id_type=MESH)
 
-    greet(sibling)
+    for t in range(owners - 1, 0, -1):
+        greet((dp, plane(t)))
     greet(along(1))
     greet(along(-1))
-    for t in range(1, owners):
-        greet((dp, plane(t)))
+    greet(sibling)
 
     def remote(src, dst, send, recv, device):
         return pltpu.make_async_remote_copy(
@@ -120,7 +124,7 @@
 
     swap = remote(xin_ref, sibx, sx_send, sx_recv, sibling)
     swap.start()
-    for t in range(1, owners):
+    for t in range(owners - 1, 0, -1):
         j = plane(t)
         remote(codes.at[0], codes.at[t], c1_send, c1_recv, (dp, j)).start()
         remote(
@@ -207,7 +211,7 @@
                 row_high == (code >> 10).astype(F32).astype(BF), jnp.concatenate([rbuf[t]] * 8, axis=0), zero
             ))
         total = dot(jnp.concatenate(left, axis=1), jnp.concatenate(right, axis=1), NT)
-        acc[...] = total if g == 0 else acc[...] + total
+        acc[...] = total if g == groups - 1 else acc[...] + total
 
     todo = list(range(1, steps + 1))
 
@@ -217,11 +221,11 @@
 
     inputs_on(3)
     arrived(codes.at[pl.ds(1, owners - 1)], c1_recv)
-    for g in range(groups):
+    for g in range(groups - 1, -1, -1):
         first = 1 if g == 0 else 0
         arrived(rbuf.at[pl.ds(8 * g + first, 8 - first)], a1_recv.at[g])
         sum_group(g)
-        if g == 0:
+        if g == groups - 1:
             inputs_on(1)
     obuf[...] = acc[...].astype(BF)
 
@@ -234,7 +238,7 @@
             pl.ds(pl.multiple_of((o // 2) * 16, 16), 16), pl.ds(pl.multiple_of((o % 2) * 128, 128), 128)
         ]
 
-    for t in range(1, owners):
+    for t in range(owners - 1, 0, -1):
         o = plane(t)
         remote(sums_of(o), place, a2_send, a2_recv, (dp, o)).start()
     pltpu.make_async_copy(sums_of(ow), place, a2_recv).start()
@@ -286,12 +290,11 @@
     sibling_part(1, gs, 1)
 
     band = width // nx
-    px, py = ow // ny, ow % ny
 
     def send_partial(w, value):
         for b in range(width // wide):
             pt[w, b * wide:(b + 1) * wide, :] = flip(value[:, b * wide:(b + 1) * wide].astype(BF))
-        for i in range(1, nx):
+        for i in far_first(nx):
             xx = lax.rem(px + i, nx)
             remote(
                 pt.at[w, pl.ds(pl.multiple_of(xx * band, band), band)], cx.at[w, i - 1],
@@ -305,7 +308,7 @@
             total = total + cx[w, i - 1].astype(F32)
         full[w] = total
         s1[w] = total.astype(BF)
-        for i in range(1, ny):
+        for i in far_first(ny):
             yy = lax.rem(py + i, ny)
             remote(
                 s1.at[w, pl.ds(pl.multiple_of(yy * share, share), share)], cy.at[w, i - 1],

time: 89.8 us -> 87.8 us (0.978)
  Pallas kernels: 87 us -> 85 us
    pallas_call x1, Pallas kernels: 87 us -> 85 us  [on_device(): pl.pallas_call(functools.partial(kernel, cfg), out_shape=(jax.ShapeDtypeS...]
where the time goes in v4:
time: 87.8 us; the launch traced here: 87.6 us
  Pallas kernels  85 us (97%)
  local copies, waits for them, and re-layouts  1.94 us (2%)
    pallas_call x1, Pallas kernels, on_device(): pl.pallas_call(functools.partial(kernel, cfg), out_shape=(jax.ShapeDtypeS...  85 us
    unnamed x4, local copies, waits for them, and re-layouts  1.94 us

profile of v4, /device:TPU:1, one launch (start us, length us, event | category | flops | bytes accessed | tf_op | source)
XLA Modules:
  0.0 87.6 jit_solution(2199542491435276952)
XLA Ops:
  0.6 85.0 %ngram_backward.1 = (f32[32,128]{1,0:T(8,128)}, f32[32,128]{1,0:T(8,128)}) custom-call(bf16[256,1024]{1,0:T(8,128)(2,1)} %rows_hbm.1, s32[1,256]{1,0:T(1,128)} %bitcast.4, s32[1,256]{1,0:T(1,128)} %bitcast.5, bf16[40,1024]{1,0:T(8,128)(2,1)} %xin_hbm.1, bf16[1024,128]{1,0:T(8,128)(2,1)} %up_hbm.1, bf16[128,1024]{1,0:T(8,128)(2,1)} %down_hbm.1), custom_call_target="tpu_custom_call" | custom-call | tf_op jit(solution)/shard_map/ngram_backward/pallas_call | solution.py:358
  85.7 0.0 copy-start
  85.7 1.3 %copy.10 = f32[32,128]{1,0:T(8,128)} copy(f32[32,128]{1,0:T(8,128)} %get-tuple-element.8) | data formatting | bytes 32768
  87.0 0.0 copy-done
  87.0 0.6 copy.11
Async XLA Ops:
  85.7 1.3 %copy-start = (f32[32,128]{1,0:T(8,128)S(1)}, f32[32,128]{1,0:T(8,128)}, u32[]{:S(2)}) copy-start(f32[32,128]{1,0:T(8,128)} %get-tuple-element.5) | copy-start | bytes 49156
